TPU v7x, 32 devices: a whole 2x2x4 slice. The times are simulated.
32 devices in a mesh: blk: 16 (over z, y, core), grp: 2 (over x).
Axes of the slice: x: 2, y: 2, z: 4, core: 2. Of those that a mesh axis runs over, the one named last changes fastest.
Arguments:
- occupied: bfloat16 [2048, 1024], P('blk'), may hold values from -6 to 6
- integrals: bfloat16 [16, 2, 3, 64, 4096], P('blk', 'grp'), may hold values from -0.75 to 0.75
- metric_inv: bfloat16 [16384, 1024], P('blk')
- pattern: int32 [16, 2, 3, 4], P('blk', 'grp'), may hold values from 0 to 15, as said below
- support: int32 [16, 8], P('blk'), may hold values from 0 to 1023, as said below
Outputs:
- exchange: float32 [2048, 128], P(('blk', 'grp'))
Inputs may be any that keep to these rules, and one draw needn't show every extreme that they name: Field 0 of every slot of pattern[r, g] is a region within distance 3 of r along the closed chain of 16 regions; field 1 is below 2; field 2 is below 16; field 3 is 1 on a leading run of slots and 0 after it, and in every draw some basis block has all 3 slots live. `support`: the 8 orbitals of one region are distinct.
All inputs are finite; a program needn't handle non-finite values.
Results may differ from a plain program's by a relative error of at most 0.0045.
Values may be sent and summed in bfloat16 or wider, within the bound.
A program may use at most 64 MiB of HBM per device.

v0:
```python
import jax
import jax.numpy as jnp
from jax import lax
from jax.sharding import PartitionSpec as P

BF = 64
AB = 64
AUXR = 1024
OSUP = 8
REACH = 3


def passed_along(value, axis, steps):
    count = lax.axis_size(axis)
    pairs = [(source, (source + steps) % count) for source in range(count)]
    return lax.ppermute(value, axis, pairs)


def per_device(occupied, integrals, metric_inv, pattern, support):
    regions = lax.axis_size("blk")
    my_region = lax.axis_index("blk")
    basis_rows = occupied.shape[0]
    orbitals = support[0]
    lower_list = []
    upper_list = []
    going_up = occupied
    going_down = occupied
    for hop_index in range(REACH):
        going_up = passed_along(going_up, "blk", 1)
        going_down = passed_along(going_down, "blk", -1)
        lower_list.append(going_up)
        upper_list.append(going_down)
    ordered = lower_list[::-1] + [occupied] + upper_list
    window = jnp.stack(ordered, 0)
    column_pick = (
        jnp.arange(occupied.shape[1], dtype=jnp.int32)[:, None] == orbitals[None, :]
    ).astype(jnp.bfloat16)
    selected = jnp.einsum(
        "wrn,ns->wrs", window, column_pick, preferred_element_type=jnp.float32
    ).astype(jnp.bfloat16)
    mu_blocks = basis_rows // BF
    block_stack = selected.reshape(-1, BF, OSUP)
    slot_fields = pattern[0, 0]
    offset_index = (slot_fields[:, 0] - my_region + regions + REACH) % regions
    block_index = offset_index * mu_blocks + slot_fields[:, 1]
    lookup = (
        block_index[:, None] == jnp.arange(block_stack.shape[0], dtype=jnp.int32)[None, :]
    ).astype(jnp.bfloat16)
    tile_rows = jnp.einsum(
        "tj,jmi->tmi", lookup, block_stack, preferred_element_type=jnp.float32
    ).astype(jnp.bfloat16)
    products = jnp.einsum(
        "tmi,tmx->tix", tile_rows, integrals[0, 0], preferred_element_type=jnp.float32
    )
    aux_blocks = AUXR // AB
    weights = (slot_fields[:, 2:3] == jnp.arange(aux_blocks, dtype=jnp.int32)[None, :]).astype(
        jnp.float32
    )
    weights = weights * slot_fields[:, 3:4].astype(jnp.float32)
    summed = jnp.einsum("ta,tix->aix", weights, products)
    half_coef = (
        summed.reshape(aux_blocks, OSUP, BF, AB).transpose(1, 2, 0, 3).reshape(OSUP, BF, AUXR)
    )
    half_coef = half_coef.astype(jnp.bfloat16)
    fitted = jnp.einsum(
        "inp,pq->inq", half_coef, metric_inv, preferred_element_type=jnp.float32
    ).astype(jnp.bfloat16)
    return jnp.einsum(
        "inq,imq->nm",
        half_coef,
        lax.all_gather(fitted, "grp", axis=1, tiled=True),
        preferred_element_type=jnp.float32,
    )


def solution(mesh):
    placed = (
        P("blk", None),
        P("blk", "grp", None, None, None),
        P("blk", None),
        P("blk", "grp", None, None),
        P("blk", None),
    )
    return jax.shard_map(
        per_device, mesh=mesh, in_specs=placed, out_specs=P(("blk", "grp"), None), check_vma=False
    )
```

profile of v0, /device:TPU:0, one launch (start us, length us, event | category | flops | bytes accessed | tf_op | source)
XLA Modules:
  0.0 95.9 jit_solution(10222339825635615082)
XLA Ops:
  6.5 0.0 all-gather.2.cloned.1.call-start
  6.5 0.5 collective-permute-start
  7.0 5.0 %collective-permute-start.3 = (bf16[128,1024]{1,0:T(8,128)(2,1)}, bf16[128,1024]{1,0:T(8,128)(2,1)S(1)}, u32[]{:S(2)}, u32[]{:S(2)}) collective-permute-start(bf16[128,1024]{1,0:T(8,128)(2,1)} %param.5), channel_id=1, source_target_pairs={{0,30},{2,0},{4,2},{6,4},{8,6},{10,8},{12,10},{14,12},{16,14},{18,... | collective-permute-start | bytes 786440 | tf_op jit(solution)/shard_map/ppermute | solution.py:16
  12.0 4.4 %collective-permute-done = bf16[128,1024]{1,0:T(8,128)(2,1)S(1)} collective-permute-done((bf16[128,1024]{1,0:T(8,128)(2,1)}, bf16[128,1024]{1,0:T(8,128)(2,1)S(1)}, u32[]{:S(2)}, u32[]{:S(2)}) %collective-permute-start) | collective-permute-done | bytes 262176 | tf_op jit(solution)/shard_map/ppermute | solution.py:16
  16.4 0.0 collective-permute-start.1
  16.4 0.0 collective-permute-done.3
  16.4 4.4 %collective-permute-start.4 = (bf16[128,1024]{1,0:T(8,128)(2,1)S(1)}, bf16[128,1024]{1,0:T(8,128)(2,1)S(1)}, u32[]{:S(2)}, u32[]{:S(2)}) collective-permute-start(bf16[128,1024]{1,0:T(8,128)(2,1)S(1)} %collective-permute-done.3), channel_id=1, source_target_pairs={{0,30},{2,0},{4,2},{6,4},{8,6},{10,8},{12,10},{14,12},{16,14},{18,... | collective-permute-start | bytes 786440 | tf_op jit(solution)/shard_map/ppermute | solution.py:16
  20.8 4.2 %collective-permute-done.1 = bf16[128,1024]{1,0:T(8,128)(2,1)S(1)} collective-permute-done((bf16[128,1024]{1,0:T(8,128)(2,1)S(1)}, bf16[128,1024]{1,0:T(8,128)(2,1)S(1)}, u32[]{:S(2)}, u32[]{:S(2)}) %collective-permute-start.1) | collective-permute-done | bytes 262176 | tf_op jit(solution)/shard_map/ppermute | solution.py:16
  25.0 0.0 collective-permute-start.2
  25.0 0.7 copy.15
  25.6 0.2 convert_reduce_fusion
  25.8 0.2 slice_reduce_fusion
  26.0 0.0 copy-start.1
  26.1 0.0 collective-permute-done.4
  26.1 4.5 %collective-permute-start.5 = (bf16[128,1024]{1,0:T(8,128)(2,1)S(1)}, bf16[128,1024]{1,0:T(8,128)(2,1)S(1)}, u32[]{:S(2)}, u32[]{:S(2)}) collective-permute-start(bf16[128,1024]{1,0:T(8,128)(2,1)S(1)} %collective-permute-done.4), channel_id=1, source_target_pairs={{0,30},{2,0},{4,2},{6,4},{8,6},{10,8},{12,10},{14,12},{16,14},{18,... | collective-permute-start | bytes 786440 | tf_op jit(solution)/shard_map/ppermute | solution.py:16
  30.6 3.0 %collective-permute-done.2 = bf16[128,1024]{1,0:T(8,128)(2,1)S(1)} collective-permute-done((bf16[128,1024]{1,0:T(8,128)(2,1)S(1)}, bf16[128,1024]{1,0:T(8,128)(2,1)S(1)}, u32[]{:S(2)}, u32[]{:S(2)}) %collective-permute-start.2) | collective-permute-done | bytes 262176 | tf_op jit(solution)/shard_map/ppermute | solution.py:16
  33.6 1.0 %bitcast_dynamic-update-slice_fusion.3 = bf16[7,128,1024]{2,1,0:T(8,128)(2,1)S(1)} fusion(bf16[7,128,1024]{2,1,0:T(8,128)(2,1)S(1)} %bitcast_dynamic-update-slice_fusion.4, bf16[128,1024]{1,0:T(8,128)(2,1)} %param.5), kind=kLoop, calls=%fused_computation.12 | loop fusion | bytes 524288
  34.7 0.0 collective-permute-done.5
  34.7 0.0 copy-done.1
  34.7 0.6 convolution_convert_fusion.1
  35.3 0.1 reshape.7
  35.4 0.2 fusion.19
  35.6 0.1 copy.9
  35.7 1.8 %fusion.2 = bf16[3,8,4096]{2,1,0:T(8,128)(2,1)S(1)} fusion(bf16[1,1,3,64,4096]{4,3,2,1,0:T(8,128)(2,1)} %param.6, bf16[3,64,8]{2,1,0:T(8,128)(2,1)S(1)} %copy.9), kind=kOutput, calls=%fused_computation.3 | convolution fusion | flops 12582912 | bytes 1772544 | tf_op jit(solution)/shard_map/tmi,tmx->tix/dot_general | solution.py:52
  37.5 0.6 convolution_convert_fusion
  38.1 3.3 %convert_element_type.31 = bf16[16,8,64,64]{3,2,0,1:T(8,128)(2,1)} reshape(bf16[16,8,4096]{2,0,1:T(8,128)(2,1)S(1)} %convolution_convert_fusion) | data formatting | bytes 2097152 | tf_op jit(solution)/shard_map/convert_element_type | solution.py:64
  41.4 4.3 %copy.8 = bf16[8,64,16,64]{3,2,1,0:T(8,128)(2,1)} copy(bf16[8,64,16,64]{3,1,2,0:T(8,128)(2,1)} %bitcast.50) | data formatting | bytes 2097152 | tf_op jit(solution)/shard_map/convert_element_type | solution.py:64
  45.7 3.2 %convert_element_type.33 = bf16[8,64,1024]{2,1,0:T(8,128)(2,1)S(1)} reshape(bf16[8,64,16,64]{3,2,1,0:T(8,128)(2,1)} %copy.8) | data formatting | bytes 2097152 | tf_op jit(solution)/shard_map/convert_element_type | solution.py:64
  48.9 2.3 %fusion.4 = bf16[8,64,1024]{2,1,0:T(8,128)(2,1)} fusion(bf16[8,64,1024]{2,1,0:T(8,128)(2,1)S(1)} %convert_element_type.33, bf16[1024,1024]{1,0:T(8,128)(2,1)S(1)} %copy-done), kind=kOutput, calls=%fused_computation.5 | convolution fusion | flops 1074266112 | bytes 4194304 | tf_op jit(solution)/shard_map/inp,pq->inq/dot_general | solution.py:65
  51.2 0.0 all-gather.2.cloned.1.call-update
  51.2 34.8 %all-gather.2.cloned.1.call-done = bf16[8,128,1024]{2,1,0:T(8,128)(2,1)} async-done(((bf16[8,64,1024]{2,1,0:T(8,128)(2,1)}), bf16[8,128,1024]{2,1,0:T(8,128)(2,1)}) %all-gather.2.cloned.1.call-update) | async-done | bytes 2097168 | tf_op jit(solution)/shard_map/all_gather | solution.py:71
  86.0 3.1 %convolution_bitcast_fusion = f32[64,128]{1,0:T(8,128)} fusion(bf16[8,64,1024]{2,1,0:T(8,128)(2,1)S(1)} %convert_element_type.33, bf16[8,128,1024]{2,1,0:T(8,128)(2,1)} %all-gather.2.cloned.1.call-done), kind=kOutput, calls=%fused_computation.6 | convolution fusion | flops 134217728 | bytes 3178496 | tf_op jit(solution)/shard_map/inq,imq->nm/dot_general | solution.py:68
  (9 shorter events, 0.1 us)
Async XLA Ops:
  6.5 42.4 %copy-start = (bf16[1024,1024]{1,0:T(8,128)(2,1)S(1)}, bf16[1024,1024]{1,0:T(8,128)(2,1)}, u32[]{:S(2)}) copy-start(bf16[1024,1024]{1,0:T(8,128)(2,1)} %param.7) | copy-start | bytes 6291460
  6.5 79.5 %all-gather.2.cloned.1.call-start = ((), (), s32[]{:S(2)}) async-start(), calls=%async_computation | async-start | bytes 3145728 | tf_op jit(solution)/shard_map/all_gather | solution.py:71
  6.5 9.8 %collective-permute-start = (bf16[128,1024]{1,0:T(8,128)(2,1)}, bf16[128,1024]{1,0:T(8,128)(2,1)S(1)}, u32[]{:S(2)}, u32[]{:S(2)}) collective-permute-start(bf16[128,1024]{1,0:T(8,128)(2,1)} %param.5), channel_id=1, source_target_pairs={{0,2},{2,4},{4,6},{6,8},{8,10},{10,12},{12,14},{14,16},{16,18},{18... | collective-permute-start | bytes 786440 | tf_op jit(solution)/shard_map/ppermute | solution.py:16
  7.0 9.4 %collective-permute-start.3 = (bf16[128,1024]{1,0:T(8,128)(2,1)}, bf16[128,1024]{1,0:T(8,128)(2,1)S(1)}, u32[]{:S(2)}, u32[]{:S(2)}) collective-permute-start(bf16[128,1024]{1,0:T(8,128)(2,1)} %param.5), channel_id=1, source_target_pairs={{0,30},{2,0},{4,2},{6,4},{8,6},{10,8},{12,10},{14,12},{16,14},{18,... | collective-permute-start | bytes 786440 | tf_op jit(solution)/shard_map/ppermute | solution.py:16
  16.4 8.6 %collective-permute-start.1 = (bf16[128,1024]{1,0:T(8,128)(2,1)S(1)}, bf16[128,1024]{1,0:T(8,128)(2,1)S(1)}, u32[]{:S(2)}, u32[]{:S(2)}) collective-permute-start(bf16[128,1024]{1,0:T(8,128)(2,1)S(1)} %collective-permute-done), channel_id=1, source_target_pairs={{0,2},{2,4},{4,6},{6,8},{8,10},{10,12},{12,14},{14,16},{16,18},{18... | collective-permute-start | bytes 786440 | tf_op jit(solution)/shard_map/ppermute | solution.py:16
  16.4 9.7 %collective-permute-start.4 = (bf16[128,1024]{1,0:T(8,128)(2,1)S(1)}, bf16[128,1024]{1,0:T(8,128)(2,1)S(1)}, u32[]{:S(2)}, u32[]{:S(2)}) collective-permute-start(bf16[128,1024]{1,0:T(8,128)(2,1)S(1)} %collective-permute-done.3), channel_id=1, source_target_pairs={{0,30},{2,0},{4,2},{6,4},{8,6},{10,8},{12,10},{14,12},{16,14},{18,... | collective-permute-start | bytes 786440 | tf_op jit(solution)/shard_map/ppermute | solution.py:16
  25.0 8.6 %collective-permute-start.2 = (bf16[128,1024]{1,0:T(8,128)(2,1)S(1)}, bf16[128,1024]{1,0:T(8,128)(2,1)S(1)}, u32[]{:S(2)}, u32[]{:S(2)}) collective-permute-start(bf16[128,1024]{1,0:T(8,128)(2,1)S(1)} %collective-permute-done.1), channel_id=1, source_target_pairs={{0,2},{2,4},{4,6},{6,8},{8,10},{10,12},{12,14},{14,16},{16,18},{18... | collective-permute-start | bytes 786440 | tf_op jit(solution)/shard_map/ppermute | solution.py:16
  26.0 8.7 %copy-start.1 = (s32[1,8]{1,0:T(1,128)S(1)}, s32[1,8]{1,0:T(1,128)}, u32[]{:S(2)}) copy-start(s32[1,8]{1,0:T(1,128)} %param.9) | copy-start | bytes 100
  26.1 8.6 %collective-permute-start.5 = (bf16[128,1024]{1,0:T(8,128)(2,1)S(1)}, bf16[128,1024]{1,0:T(8,128)(2,1)S(1)}, u32[]{:S(2)}, u32[]{:S(2)}) collective-permute-start(bf16[128,1024]{1,0:T(8,128)(2,1)S(1)} %collective-permute-done.4), channel_id=1, source_target_pairs={{0,30},{2,0},{4,2},{6,4},{8,6},{10,8},{12,10},{14,12},{16,14},{18,... | collective-permute-start | bytes 786440 | tf_op jit(solution)/shard_map/ppermute | solution.py:16
Sparse Core Ops, SparseCore 0:
  51.3 34.6 all-gather.1
where the time goes:
time: 96.2 us; the launch traced here: 95.9 us
  waiting for transfers between devices  46.4 us (48%)
  starting transfers between devices  14.4 us (15%)
  between operations  13.5 us (14%)
  local copies, waits for them, and re-layouts  12.8 us (13%)
  matrix products  8.45 us (9%)
    all_gather x1, waiting for transfers between devices, per_device(): lax.all_gather(fitted, 'grp', axis=1, tiled=True)  34.8 us
    ppermute x6, starting transfers between devices, passed_along(): return lax.ppermute(value, axis, pairs)  14.4 us
    ppermute x6, waiting for transfers between devices, passed_along(): return lax.ppermute(value, axis, pairs)  11.5 us
    convert_element_type x3, local copies, waits for them, and re-layouts, per_device(): half_coef = half_coef.astype(jnp.bfloat16)  10.8 us
    dot_general x1, matrix products, per_device(): jnp.einsum('inq,imq->nm', half_coef, lax.all_gather(fitted, 'grp', axis=1...  3.05 us
    dot_general x1, matrix products, per_device(): jnp.einsum('inp,pq->inq', half_coef, metric_inv, preferred_element_type=j...  2.25 us
  transfers between devices with their start and end apart: 7, of which 4 were waited for; matrix products, arithmetic and copies ran while one was open for 2% of the time, Pallas kernels for 0%

commit v1 on v0

v1 whole, which is shorter than its diff:
```python
import functools

import jax
import jax.numpy as jnp
from jax import lax
from jax.experimental import pallas as pl
from jax.experimental.pallas import tpu as pltpu
from jax.sharding import PartitionSpec as P

BF = 64
AB = 64
AUXR = 1024
OSUP = 8
REACH = 3
LANES = 128
PAIR = LANES // BF
HALF = OSUP // PAIR
NEAR = tuple(d for d in range(-REACH, REACH + 1) if d != 0)
MESH = pl.DeviceIdType.MESH
NT_DIMS = (((1,), (1,)), ((), ()))


def iota(shape, dim):
    return lax.broadcasted_iota(jnp.int32, shape, dim)


def splat_rows(values):
    rows = iota((8, LANES), 0)
    tile = jnp.zeros((8, LANES), jnp.int32)
    for at, value in enumerate(values):
        tile = jnp.where(rows == at, value, tile)
    return tile


def kernel(
    regions, groups, occ_hbm, int_hbm, met_hbm, pat, sup, out_ref,
    occ, ints, met, mcol, m2, kbuf, my_sup, my_pat, sups, pats, picked, sel,
    comp, mixed, half, blocks,
    load_sem, sup_send, sup_recv, pat_send, pat_recv, sel_send, sel_recv, half_send, half_recv,
):
    slots = int_hbm.shape[2]
    rows = occ.shape[0]
    me = lax.axis_index("blk")
    mine = lax.axis_index("grp")
    near = [lax.rem(me + (d + regions), regions) for d in NEAR]
    peers = [lax.rem(mine + j, groups) for j in range(1, groups)]
    count = len(NEAR)

    loads = [
        pltpu.make_async_copy(occ_hbm, occ, load_sem.at[0]),
        pltpu.make_async_copy(met_hbm, met, load_sem.at[1]),
    ]
    for t in range(slots):
        loads.append(
            pltpu.make_async_copy(int_hbm.at[0, 0, t], ints.at[pl.ds(t * BF, BF)], load_sem.at[2 + t])
        )

    barrier = pltpu.get_barrier_semaphore()
    for region in near:
        pl.semaphore_signal(barrier, inc=1, device_id={"blk": region}, device_id_type=MESH)
    for peer in peers:
        pl.semaphore_signal(barrier, inc=1, device_id={"grp": peer}, device_id_type=MESH)
    for load in loads:
        load.start()

    aux = [pat[t, 0, 2] for t in range(slots)]
    my_sup[...] = splat_rows([sup[0, i] for i in range(OSUP)])
    my_pat[...] = splat_rows(aux)
    pats[0] = my_pat[...]
    pl.semaphore_wait(barrier, count + groups - 1)

    sup_out, pat_out = [], []
    for k, region in enumerate(near):
        copy = pltpu.make_async_remote_copy(
            src_ref=my_sup, dst_ref=sups.at[count - 1 - k], send_sem=sup_send.at[k],
            recv_sem=sup_recv.at[count - 1 - k], device_id={"blk": region}, device_id_type=MESH,
        )
        copy.start()
        sup_out.append(copy)
    for j, peer in enumerate(peers):
        copy = pltpu.make_async_remote_copy(
            src_ref=my_pat, dst_ref=pats.at[groups - 1 - j], send_sem=pat_send.at[j],
            recv_sem=pat_recv.at[groups - 2 - j], device_id={"grp": peer}, device_id_type=MESH,
        )
        copy.start()
        pat_out.append(copy)

    loads[1].wait()
    tall = iota((AUXR, LANES), 0)
    wide = iota((1, LANES), 1) % AB
    pick = jnp.concatenate(
        [(tall == aux[t] * AB + wide).astype(jnp.float32) for t in range(slots)], axis=1
    ).astype(jnp.bfloat16)
    mcol[...] = jnp.dot(met[...], pick, preferred_element_type=jnp.float32).astype(jnp.bfloat16)

    def one_hot(tile):
        lane = iota((8, LANES), 1)
        parts = [(lane + c * LANES == tile).astype(jnp.float32) for c in range(occ.shape[1] // LANES)]
        return jnp.concatenate(parts, axis=1)

    loads[0].wait()
    for k in range(count):
        sup_out[k].wait_recv()
    hot = jnp.concatenate([one_hot(sups[k]) for k in range(count)] + [one_hot(my_sup[...])], axis=0)
    chosen = lax.dot_general(
        hot.astype(jnp.bfloat16), occ[...], NT_DIMS, preferred_element_type=jnp.float32
    )
    for k in range(count):
        picked[k] = chosen[k * OSUP:(k + 1) * OSUP]
    sel[REACH] = chosen[count * OSUP:(count + 1) * OSUP]
    sel_out = []
    for k, region in enumerate(near):
        at = REACH - NEAR[k]
        copy = pltpu.make_async_remote_copy(
            src_ref=picked.at[k], dst_ref=sel.at[at], send_sem=sel_send.at[k],
            recv_sem=sel_recv.at[count - 1 - k], device_id={"blk": region}, device_id_type=MESH,
        )
        copy.start()
        sel_out.append(copy)

    lane64 = iota((AB, LANES), 1)
    row64 = iota((AB, LANES), 0)
    side = (iota((AB, slots * LANES), 1) // AB) % PAIR
    for j in range(groups):
        if j > 0:
            pat_out[groups - 1 - j].wait_recv()
        for t in range(slots):
            start = pats[j, t:t + 1, :] * AB
            hot_rows = jnp.concatenate(
                [
                    (lane64 + (c * LANES) - start == row64).astype(jnp.float32)
                    for c in range(AUXR // LANES)
                ],
                axis=1,
            ).astype(jnp.bfloat16)
            block = jnp.dot(hot_rows, mcol[...], preferred_element_type=jnp.float32)
            for b in range(PAIR):
                at = (t * PAIR + b) * AB
                m2[j, at:at + AB, :] = jnp.where(side == b, block, 0.0).astype(jnp.bfloat16)

    for k in range(count):
        pltpu.make_async_remote_copy(
            src_ref=picked.at[k], dst_ref=sel.at[REACH + NEAR[k]], send_sem=sel_send.at[k],
            recv_sem=sel_recv.at[k], device_id={"blk": near[k]}, device_id_type=MESH,
        ).wait_recv()
    tiles = []
    for t in range(slots):
        source = lax.rem(pat[t, 0, 0] - me + (regions + REACH), regions)
        place = source * (rows // BF) + pat[t, 0, 1]
        evens = jnp.zeros((OSUP, LANES), jnp.float32)
        odds = evens
        for w in range(count + 1):
            for c in range(rows // LANES):
                at = w * (rows // BF) + c * PAIR
                part = sel[w, :, c * LANES:(c + 1) * LANES]
                evens = jnp.where(place == at, part, evens)
                odds = jnp.where(place == at + 1, part, odds)
        tiles.append(evens[:, :BF] + odds[:, BF:])
    mix = []
    for t in range(slots):
        first = jnp.float32(1.0)
        for u in range(t):
            first = jnp.where(aux[u] == aux[t], jnp.float32(0.0), first)
        line = []
        for u in range(slots):
            live = pat[u, 0, 3].astype(jnp.float32)
            line.append(tiles[u] * (jnp.where(aux[u] == aux[t], live, jnp.float32(0.0)) * first))
        mix.append(jnp.concatenate(line, axis=1))
    mix = jnp.concatenate(mix, axis=0).astype(jnp.bfloat16)
    for load in loads[2:]:
        load.wait()
    width = 512
    for n in range(ints.shape[1] // width):
        part = jnp.dot(mix, ints[:, n * width:(n + 1) * width], preferred_element_type=jnp.float32)
        for c in range(width // LANES):
            at = (n * (width // LANES) + c) * OSUP
            for t in range(slots):
                comp[t, at:at + OSUP, :] = part[
                    t * OSUP:(t + 1) * OSUP, c * LANES:(c + 1) * LANES
                ]

    pairs = BF // PAIR
    low = iota((pairs, LANES), 1) < AB
    half_out = []
    for t in range(slots):
        for i in range(HALF):
            at = (t * HALF + i) * BF
            a = comp[t, pl.ds(i, pairs, stride=OSUP), :]
            b = comp[t, pl.ds(i + HALF, pairs, stride=OSUP), :]
            mixed[pl.ds(at, pairs, stride=PAIR), :] = jnp.where(low, a, pltpu.roll(b, AB, 1))
            mixed[pl.ds(at + 1, pairs, stride=PAIR), :] = jnp.where(low, pltpu.roll(a, AB, 1), b)
        span = pl.ds(t * HALF * BF, HALF * BF)
        half[mine, span, :] = mixed[span, :].astype(jnp.bfloat16)
        for j, peer in enumerate(peers):
            copy = pltpu.make_async_remote_copy(
                src_ref=half.at[mine, span], dst_ref=half.at[mine, span],
                send_sem=half_send.at[t, j], recv_sem=half_recv.at[t, groups - 2 - j],
                device_id={"grp": peer}, device_id_type=MESH,
            )
            copy.start()
            half_out.append(copy)

    own = jnp.concatenate(
        [half[mine, pl.ds(t * HALF * BF, HALF * BF), :] for t in range(slots)], axis=1
    )

    def against(j, t, other):
        left = jnp.concatenate(
            [
                kbuf[j, i * BF:(i + 1) * BF, t * LANES:(t + 1) * LANES]
                for i in range(HALF)
            ],
            axis=1,
        )
        right = jnp.concatenate(
            [
                half[other, pl.ds((t * HALF + i) * BF, BF), :]
                for i in range(HALF)
            ],
            axis=1,
        )
        return lax.dot_general(left, right, NT_DIMS, preferred_element_type=jnp.float32)

    for j in range(groups):
        kbuf[j] = lax.dot_general(
            own, m2[j], NT_DIMS, preferred_element_type=jnp.float32
        ).astype(jnp.bfloat16)
    blocks[0] = sum(against(0, t, mine) for t in range(slots))
    for j in range(1, groups):
        other = lax.rem(mine + j, groups)
        total = None
        for t in range(slots):
            span = pl.ds(t * HALF * BF, HALF * BF)
            pltpu.make_async_remote_copy(
                src_ref=half.at[mine, span], dst_ref=half.at[other, span],
                send_sem=half_send.at[t, j - 1], recv_sem=half_recv.at[t, j - 1],
                device_id={"grp": peers[j - 1]}, device_id_type=MESH,
            ).wait_recv()
            term = against(j, t, other)
            total = term if total is None else total + term
        blocks[j] = total
    out_ref[...] = jnp.concatenate(
        [blocks[lax.rem(h - mine + groups, groups)] for h in range(groups)], axis=1
    )
    for copy in sup_out + pat_out + sel_out + half_out:
        copy.wait_send()


def per_device(regions, groups, occupied, integrals, metric_inv, pattern, support):
    rows = occupied.shape[0]
    slots = integrals.shape[2]
    count = len(NEAR)
    tall = slots * OSUP * BF // PAIR
    dma = pltpu.SemaphoreType.DMA
    return pl.pallas_call(
        functools.partial(kernel, regions, groups),
        out_shape=jax.ShapeDtypeStruct((BF, groups * BF), jnp.float32),
        in_specs=[pl.BlockSpec(memory_space=pl.ANY)] * 3
        + [pl.BlockSpec(memory_space=pltpu.SMEM)] * 2,
        out_specs=pl.BlockSpec(memory_space=pltpu.VMEM),
        scratch_shapes=[
            pltpu.VMEM(occupied.shape, jnp.bfloat16),
            pltpu.VMEM((slots * BF, integrals.shape[4]), jnp.bfloat16),
            pltpu.VMEM(metric_inv.shape, jnp.bfloat16),
            pltpu.VMEM((AUXR, slots * LANES), jnp.bfloat16),
            pltpu.VMEM((groups, slots * LANES, slots * LANES), jnp.bfloat16),
            pltpu.VMEM((groups, HALF * BF, slots * LANES), jnp.bfloat16),
            pltpu.VMEM((8, LANES), jnp.int32),
            pltpu.VMEM((8, LANES), jnp.int32),
            pltpu.VMEM((count, 8, LANES), jnp.int32),
            pltpu.VMEM((groups, 8, LANES), jnp.int32),
            pltpu.VMEM((count, OSUP, rows), jnp.float32),
            pltpu.VMEM((count + 1, OSUP, rows), jnp.float32),
            pltpu.VMEM((slots, OSUP * BF // PAIR, LANES), jnp.float32),
            pltpu.VMEM((tall, LANES), jnp.float32),
            pltpu.VMEM((groups, tall, LANES), jnp.bfloat16),
            pltpu.VMEM((groups, BF, BF), jnp.float32),
            dma((2 + slots,)),
            dma((count,)),
            dma((count,)),
            dma((groups - 1,)),
            dma((groups - 1,)),
            dma((count,)),
            dma((count,)),
            dma((slots, groups - 1)),
            dma((slots, groups - 1)),
        ],
        compiler_params=pltpu.CompilerParams(
            collective_id=0, has_side_effects=True, vmem_limit_bytes=62 * 1024 * 1024
        ),
        cost_estimate=pl.CostEstimate(flops=2 * 10**9, bytes_accessed=4 * 10**6, transcendentals=0),
    )(occupied, integrals, metric_inv, pattern.reshape(slots, 1, pattern.shape[3]), support)


def solution(mesh):
    placed = (
        P("blk", None),
        P("blk", "grp", None, None, None),
        P("blk", None),
        P("blk", "grp", None, None),
        P("blk", None),
    )
    return jax.shard_map(
        functools.partial(per_device, mesh.shape["blk"], mesh.shape["grp"]),
        mesh=mesh, in_specs=placed, out_specs=P(("blk", "grp"), None), check_vma=False,
    )
```

time: 96.2 us -> 25.1 us (0.26)
  waiting for transfers between devices: 46.4 us -> 0 us
  Pallas kernels: 0 us -> 23.6 us
  starting transfers between devices: 14.4 us -> 0 us
  between operations: 13.5 us -> 0.01 us
  local copies, waits for them, and re-layouts: 12.8 us -> 1.38 us
  matrix products: 8.45 us -> 0 us
    all_gather x1 -> x0, waiting for transfers between devices: 34.8 us -> none  [per_device(): lax.all_gather(fitted, 'grp', axis=1, tiled=True)]
    pallas_call x0 -> x1, Pallas kernels: none -> 23.6 us  [per_device(): pl.pallas_call(functools.partial(kernel, regions, groups), out_shape=jax....]
    ppermute x6 -> x0, starting transfers between devices: 14.4 us -> none  [passed_along(): return lax.ppermute(value, axis, pairs)]
    ppermute x6 -> x0, waiting for transfers between devices: 11.5 us -> none  [passed_along(): return lax.ppermute(value, axis, pairs)]
    convert_element_type x4 -> x0, local copies, waits for them, and re-layouts: 10.8 us -> none  [the longest x3 10.8 us: per_device(): half_coef = half_coef.astype(jnp.bfloat16)]
    dot_general x6 -> x0, matrix products: 8.45 us -> none  [the longest x1 3.05 us: per_device(): jnp.einsum('inq,imq->nm', half_coef, lax.all_gather(fitted, 'grp', axis=1...]
  transfers between devices with their start and end apart: 7 -> 0, of which waited for: 4 -> 0; matrix products, arithmetic and copies ran while one was open for 2% -> 0% of each run, Pallas kernels for 0% -> 0%
where the time goes in v1:
time: 25.1 us; the launch traced here: 24.9 us
  Pallas kernels  23.6 us (94%)
  local copies, waits for them, and re-layouts  1.38 us (5%)
    pallas_call x1, Pallas kernels, per_device(): pl.pallas_call(functools.partial(kernel, regions, groups), out_shape=jax....  23.6 us
    unnamed x1, local copies, waits for them, and re-layouts  1.38 us

profile of v1, /device:TPU:0, one launch (start us, length us, event | category | flops | bytes accessed | tf_op | source)
XLA Modules:
  0.0 24.9 jit_solution(3824489636855826204)
XLA Ops:
  0.0 23.6 %shard_map.55 = f32[64,128]{1,0:T(8,128)} custom-call(bf16[128,1024]{1,0:T(8,128)(2,1)} %occ_hbm.1, bf16[1,1,3,64,4096]{4,3,2,1,0:T(8,128)(2,1)} %int_hbm.1, bf16[1024,1024]{1,0:T(8,128)(2,1)} %met_hbm.1, s32[3,1,4]{2,1,0:T(1,128)} %bitcast.1, s32[1,8]{1,0:T(1,128)} %sup.1), custom_call_target="tpu_custom_call" | custom-call | flops 2000000000 | bytes 4000000 | tf_op jit(solution)/shard_map/pallas_call | solution.py:255
  23.6 1.4 %copy.7 = f32[64,128]{1,0:T(8,128)} copy(f32[64,128]{1,0:T(8,128)} %shard_map.55) | data formatting | bytes 65536

commit v2 on v1

--- a/solution.py
+++ b/solution.py
@@ -33,10 +33,10 @@
 
 
 def kernel(
-    regions, groups, occ_hbm, int_hbm, met_hbm, pat, sup, out_ref,
-    occ, ints, met, mcol, m2, kbuf, my_sup, my_pat, sups, pats, picked, sel,
+    regions, groups, occ_hbm, int_hbm, met_hbm, pat_hbm, sup_hbm, out_ref,
+    pat, sup, occ, ints, met, mcol, m2, kbuf, my_sup, my_pat, sups, pats, picked, sel,
     comp, mixed, half, blocks,
-    load_sem, sup_send, sup_recv, pat_send, pat_recv, sel_send, sel_recv, half_send, half_recv,
+    field_sem, load_sem, sup_send, sup_recv, pat_send, pat_recv, sel_send, sel_recv, half_send, half_recv,
 ):
     slots = int_hbm.shape[2]
     rows = occ.shape[0]
@@ -55,13 +55,20 @@
             pltpu.make_async_copy(int_hbm.at[0, 0, t], ints.at[pl.ds(t * BF, BF)], load_sem.at[2 + t])
         )
 
+    fields = pltpu.make_async_copy(pat_hbm, pat, field_sem.at[0])
+    orbitals = pltpu.make_async_copy(sup_hbm, sup, field_sem.at[1])
+
     barrier = pltpu.get_barrier_semaphore()
     for region in near:
         pl.semaphore_signal(barrier, inc=1, device_id={"blk": region}, device_id_type=MESH)
     for peer in peers:
         pl.semaphore_signal(barrier, inc=1, device_id={"grp": peer}, device_id_type=MESH)
+    orbitals.start()
+    fields.start()
     for load in loads:
         load.start()
+    orbitals.wait()
+    fields.wait()
 
     aux = [pat[t, 0, 2] for t in range(slots)]
     my_sup[...] = splat_rows([sup[0, i] for i in range(OSUP)])
@@ -255,10 +262,11 @@
     return pl.pallas_call(
         functools.partial(kernel, regions, groups),
         out_shape=jax.ShapeDtypeStruct((BF, groups * BF), jnp.float32),
-        in_specs=[pl.BlockSpec(memory_space=pl.ANY)] * 3
-        + [pl.BlockSpec(memory_space=pltpu.SMEM)] * 2,
+        in_specs=[pl.BlockSpec(memory_space=pl.ANY)] * 5,
         out_specs=pl.BlockSpec(memory_space=pltpu.VMEM),
         scratch_shapes=[
+            pltpu.SMEM((slots, 1, pattern.shape[3]), jnp.int32),
+            pltpu.SMEM(support.shape, jnp.int32),
             pltpu.VMEM(occupied.shape, jnp.bfloat16),
             pltpu.VMEM((slots * BF, integrals.shape[4]), jnp.bfloat16),
             pltpu.VMEM(metric_inv.shape, jnp.bfloat16),
@@ -275,6 +283,7 @@
             pltpu.VMEM((tall, LANES), jnp.float32),
             pltpu.VMEM((groups, tall, LANES), jnp.bfloat16),
             pltpu.VMEM((groups, BF, BF), jnp.float32),
+            dma((2,)),
             dma((2 + slots,)),
             dma((count,)),
             dma((count,)),

time: 25.1 us -> 24.4 us (0.972)
  Pallas kernels: 23.6 us -> 22.9 us
    pallas_call x1, Pallas kernels: 23.6 us -> 22.9 us  [per_device(): pl.pallas_call(functools.partial(kernel, regions, groups), out_shape=jax....]
where the time goes in v2:
time: 24.4 us; the launch traced here: 24.2 us
  Pallas kernels  22.9 us (94%)
  local copies, waits for them, and re-layouts  1.38 us (6%)
    pallas_call x1, Pallas kernels, per_device(): pl.pallas_call(functools.partial(kernel, regions, groups), out_shape=jax....  22.9 us
    unnamed x1, local copies, waits for them, and re-layouts  1.38 us

profile of v2, /device:TPU:0, one launch (start us, length us, event | category | flops | bytes accessed | tf_op | source)
XLA Modules:
  0.0 24.2 jit_solution(16837983075919251047)
XLA Ops:
  0.0 22.9 %shard_map.55 = f32[64,128]{1,0:T(8,128)} custom-call(bf16[128,1024]{1,0:T(8,128)(2,1)} %occ_hbm.1, bf16[1,1,3,64,4096]{4,3,2,1,0:T(8,128)(2,1)} %int_hbm.1, bf16[1024,1024]{1,0:T(8,128)(2,1)} %met_hbm.1, s32[3,1,4]{2,1,0:T(1,128)} %bitcast.1, s32[1,8]{1,0:T(1,128)} %sup_hbm.1), custom_call_target="tpu_custom_call" | custom-call | flops 2000000000 | bytes 4000000 | tf_op jit(solution)/shard_map/pallas_call | solution.py:262
  22.9 1.4 %copy.7 = f32[64,128]{1,0:T(8,128)} copy(f32[64,128]{1,0:T(8,128)} %shard_map.55) | data formatting | bytes 65536

commit v3 on v2

--- a/solution.py
+++ b/solution.py
@@ -59,7 +59,7 @@
     orbitals = pltpu.make_async_copy(sup_hbm, sup, field_sem.at[1])
 
     barrier = pltpu.get_barrier_semaphore()
-    for region in near:
+    for region in near[::-1]:
         pl.semaphore_signal(barrier, inc=1, device_id={"blk": region}, device_id_type=MESH)
     for peer in peers:
         pl.semaphore_signal(barrier, inc=1, device_id={"grp": peer}, device_id_type=MESH)
@@ -116,7 +116,7 @@
         picked[k] = chosen[k * OSUP:(k + 1) * OSUP]
     sel[REACH] = chosen[count * OSUP:(count + 1) * OSUP]
     sel_out = []
-    for k, region in enumerate(near):
+    for k, region in reversed(list(enumerate(near))):
         at = REACH - NEAR[k]
         copy = pltpu.make_async_remote_copy(
             src_ref=picked.at[k], dst_ref=sel.at[at], send_sem=sel_send.at[k],

time: 24.4 us -> 24.1 us (0.988)
  Pallas kernels: 22.9 us -> 22.5 us
    pallas_call x1, Pallas kernels: 22.9 us -> 22.5 us  [per_device(): pl.pallas_call(functools.partial(kernel, regions, groups), out_shape=jax....]
where the time goes in v3:
time: 24.1 us; the launch traced here: 23.9 us
  Pallas kernels  22.5 us (93%)
  local copies, waits for them, and re-layouts  1.38 us (6%)
    pallas_call x1, Pallas kernels, per_device(): pl.pallas_call(functools.partial(kernel, regions, groups), out_shape=jax....  22.5 us
    unnamed x1, local copies, waits for them, and re-layouts  1.38 us

profile of v3, /device:TPU:0, one launch (start us, length us, event | category | flops | bytes accessed | tf_op | source)
XLA Modules:
  0.0 23.9 jit_solution(15140749198627551058)
XLA Ops:
  0.0 22.5 %shard_map.55 = f32[64,128]{1,0:T(8,128)} custom-call(bf16[128,1024]{1,0:T(8,128)(2,1)} %occ_hbm.1, bf16[1,1,3,64,4096]{4,3,2,1,0:T(8,128)(2,1)} %int_hbm.1, bf16[1024,1024]{1,0:T(8,128)(2,1)} %met_hbm.1, s32[3,1,4]{2,1,0:T(1,128)} %bitcast.1, s32[1,8]{1,0:T(1,128)} %sup_hbm.1), custom_call_target="tpu_custom_call" | custom-call | flops 2000000000 | bytes 4000000 | tf_op jit(solution)/shard_map/pallas_call | solution.py:262
  22.6 1.4 %copy.7 = f32[64,128]{1,0:T(8,128)} copy(f32[64,128]{1,0:T(8,128)} %shard_map.55) | data formatting | bytes 65536
